TPU v7x, 32 devices: a whole 2x2x4 slice. The times are simulated.
32 devices in a mesh: seq: 4 (over y, x), fsdp: 8 (over z, core).
Axes of the slice: x: 2, y: 2, z: 4, core: 2. Of those that a mesh axis runs over, the one named last changes fastest.
Arguments:
- hidden: bfloat16 [8, 1024, 1024], P('fsdp', 'seq'), may hold values from -6 to 6
- lengths: int32 [8], P('fsdp'), may hold values from 1 to 1024, 5120 in all
- expert_ids: int32 [8, 1024, 1], P('fsdp', 'seq'), may hold values from 0 to 15; in each aligned block of 256 rows (0 to 255, 256 to 511, ..., all dimensions but the last counted through in order) at most 32 rows name the same one
- attn_gain: bfloat16 [1024], P(('seq', 'fsdp')), may hold values from 0.5 to 1.5
- qkv_weight: bfloat16 [1024, 3072], P(('seq', 'fsdp')), may hold values from -0.1875 to 0.1875
- out_weight: bfloat16 [1024, 1024], P(('seq', 'fsdp')), may hold values from -2 to 2
- moe_gain: bfloat16 [1024], P(('seq', 'fsdp')), may hold values from 0.5 to 1.5
- router_weight: bfloat16 [1024, 16], P(('seq', 'fsdp')), may hold values from -0.09375 to 0.09375
- expert_in: bfloat16 [16, 1024, 4096], P('fsdp', None, 'seq'), may hold values from -0.1875 to 0.1875
- expert_out: bfloat16 [16, 4096, 1024], P('fsdp', 'seq'), may hold values from -12 to 12
- out_grad: bfloat16 [8, 1024, 1024], P('fsdp', 'seq'), may hold values from -6 to 6
Outputs:
- output: bfloat16 [8, 1024, 1024], P('fsdp', 'seq')
- input_grad: float32 [8, 1024, 1024], P('fsdp', 'seq')
- attn_gain_grad: float32 [1024], P(('seq', 'fsdp'))
- qkv_grad: float32 [1024, 3072], P(('seq', 'fsdp'))
- out_weight_grad: float32 [1024, 1024], P(('seq', 'fsdp'))
- moe_gain_grad: float32 [1024], P(('seq', 'fsdp'))
- router_grad: float32 [1024, 16], P(('seq', 'fsdp'))
- expert_in_grad: float32 [16, 1024, 4096], P('fsdp', None, 'seq')
- expert_out_grad: float32 [16, 4096, 1024], P('fsdp', 'seq')
Inputs may be any that keep to these rules, and one draw needn't show every extreme that they name: `lengths`: the longest slot holds exactly 1024 valid positions. `expert_ids`: in each aligned block of 256 tokens (the tokens of one device, slots first, then positions), no expert is named more than 32 times, and in some block one expert is named exactly 32 times.
All inputs are finite; a program needn't handle non-finite values. No bound on the sum of `lengths` on one device may be relied on, other than what follows from the above.
Results may differ from a plain program's by a relative error of at most 0.017.
Values may be sent and summed in bfloat16 or wider, within the bound.
A program may use at most 192 MiB of HBM per device.

v0:
```python
import jax
import jax.numpy as jnp
from jax import lax
from jax.sharding import PartitionSpec as P

HEAD_DIM = 64
QBLOCK = 512
EPS = 1e-05
MASKED = -1e30


def scaled_norm(value, gain):
    return value * lax.rsqrt(jnp.mean(value * value, axis=-1, keepdims=True) + EPS) * gain


def gelu_tanh(value):
    return jax.nn.gelu(value, approximate=True)


def times_transposed(left, right):
    return lax.dot_general(
        left, right, (((1,), (1,)), ((), ())), preferred_element_type=jnp.float32
    )


def transposed_times(left, right):
    return lax.dot_general(
        left, right, (((0,), (0,)), ((), ())), preferred_element_type=jnp.float32
    )


def to_heads(value):
    return lax.all_to_all(value, "seq", split_axis=2, concat_axis=0, tiled=True)


def to_tokens(value):
    return lax.all_to_all(value, "seq", split_axis=0, concat_axis=2, tiled=True)


def to_owners(value):
    return lax.all_to_all(value, "fsdp", split_axis=0, concat_axis=0, tiled=True)


def to_sources(value):
    return lax.all_to_all(value, "fsdp", split_axis=0, concat_axis=0, tiled=True)


def spread_rows(value):
    return lax.all_gather(value, "seq", axis=2, tiled=True)


def collect_rows(value):
    return lax.psum_scatter(value, "seq", scatter_dimension=2, tiled=True)


def masked_scores(block_query, keys, start, length, scale):
    scores = (
        jnp.einsum("qhd,khd->hqk", block_query, keys, preferred_element_type=jnp.float32) * scale
    )
    rows = start + jnp.arange(block_query.shape[0], dtype=jnp.int32)
    columns = jnp.arange(keys.shape[0], dtype=jnp.int32)
    keep = (columns[None, :] <= rows[:, None]) & (columns[None, :] < length)
    return jnp.where(keep[None], scores, MASKED)


def shards(
    hidden,
    lengths,
    expert_ids,
    attn_gain,
    qkv_weight,
    out_weight,
    moe_gain,
    router_weight,
    expert_in,
    expert_out,
    out_grad,
):
    seq_count = lax.axis_size("seq")
    seq_place = lax.axis_index("seq")
    tokens = hidden.shape[1]
    width = hidden.shape[2]
    full_len = tokens * seq_count
    gain_one, weight_qkv, weight_mix, gain_two, weight_route = (
        lax.all_gather(attn_gain, ("seq", "fsdp"), axis=0, tiled=True),
        lax.all_gather(qkv_weight, ("seq", "fsdp"), axis=0, tiled=True),
        lax.all_gather(out_weight, ("seq", "fsdp"), axis=0, tiled=True),
        lax.all_gather(moe_gain, ("seq", "fsdp"), axis=0, tiled=True),
        lax.all_gather(router_weight, ("seq", "fsdp"), axis=0, tiled=True),
    )
    experts_all = weight_route.shape[1]
    expert_local = expert_in.shape[0]
    owners = experts_all // expert_local
    capacity = max(2, 2 * tokens // experts_all)
    heads_local = width // seq_count // HEAD_DIM
    group_width = width // seq_count
    scale = HEAD_DIM ** (-0.5)
    length = lengths[0]
    position = seq_place * tokens + jnp.arange(tokens, dtype=jnp.int32)
    valid = (position < length).astype(jnp.float32)[:, None]
    inputs = hidden[0].astype(jnp.float32)
    normed, norm_back = jax.vjp(scaled_norm, inputs, gain_one.astype(jnp.float32))
    normed = normed.astype(jnp.bfloat16)
    projected = jnp.dot(normed, weight_qkv, preferred_element_type=jnp.float32).astype(jnp.bfloat16)
    grouped = to_heads(projected.reshape(tokens, 3, width))
    query = grouped[:, 0].reshape(full_len, heads_local, HEAD_DIM)
    keys = grouped[:, 1].reshape(full_len, heads_local, HEAD_DIM)
    values = grouped[:, 2].reshape(full_len, heads_local, HEAD_DIM)
    starts = list(range(0, full_len, QBLOCK))
    outputs = []
    totals = []
    for start in starts:
        reach = full_len
        block_query = query[start : start + QBLOCK]
        scores = masked_scores(block_query, keys, start, length, scale)
        top = jnp.max(scores, axis=-1, keepdims=True)
        total = top + jnp.log(jnp.sum(jnp.exp(scores - top), axis=-1, keepdims=True))
        probs = jnp.exp(scores - total).astype(jnp.bfloat16)
        block_out = jnp.einsum("hqk,khd->qhd", probs, values, preferred_element_type=jnp.float32)
        outputs.append(block_out.astype(jnp.bfloat16))
        totals.append(total)
    attended = jnp.concatenate(outputs, axis=0).reshape(full_len, 1, group_width)
    mixed = to_tokens(attended).reshape(tokens, width)
    middle = inputs + jnp.dot(mixed, weight_mix, preferred_element_type=jnp.float32)
    normed_two, norm_two_back = jax.vjp(scaled_norm, middle, gain_two.astype(jnp.float32))
    normed_two = normed_two.astype(jnp.bfloat16)
    logits = jnp.dot(normed_two, weight_route, preferred_element_type=jnp.float32)
    chosen = expert_ids[0, :, 0]
    choose = chosen[:, None] == jnp.arange(experts_all, dtype=jnp.int32)[None, :]

    def gate_of(logit_rows):
        return jnp.sum(jnp.where(choose, jax.nn.softmax(logit_rows, axis=-1), 0.0), axis=-1)

    gate, gate_back = jax.vjp(gate_of, logits)
    counts = choose.astype(jnp.int32)
    ranks = jnp.sum(jnp.cumsum(counts, axis=0) * counts, axis=1) - 1
    slot = chosen * capacity + ranks
    dispatch = (
        jnp.arange(experts_all * capacity, dtype=jnp.int32)[:, None] == slot[None, :]
    ).astype(jnp.bfloat16)
    sent = jnp.dot(dispatch, normed_two, preferred_element_type=jnp.float32).astype(jnp.bfloat16)
    arrived = to_owners(sent.reshape(owners, expert_local, capacity, width))
    rows_all = spread_rows(arrived)
    weight_in, weight_out = (expert_in, expert_out)
    inner = jnp.einsum("sjcd,jdf->sjcf", rows_all, weight_in, preferred_element_type=jnp.float32)
    active, active_back = jax.vjp(gelu_tanh, inner)
    active = active.astype(jnp.bfloat16)
    partial_out = jnp.einsum(
        "sjcf,jfd->sjcd", active, weight_out, preferred_element_type=jnp.float32
    )
    produced = collect_rows(partial_out)
    returned = to_sources(produced.astype(jnp.bfloat16)).reshape(experts_all * capacity, width)
    back_rows = jnp.einsum("st,sd->td", dispatch, returned, preferred_element_type=jnp.float32)
    output = valid * (middle + gate[:, None] * back_rows)
    upstream = out_grad[0].astype(jnp.float32) * valid
    grad_returned = (upstream * gate[:, None]).astype(jnp.bfloat16)
    grad_gate = jnp.sum(upstream * back_rows, axis=1)
    grad_logits = gate_back(grad_gate)[0].astype(jnp.bfloat16)
    grad_route = transposed_times(normed_two, grad_logits)
    grad_normed_two = times_transposed(grad_logits, weight_route)
    grad_sent = jnp.dot(dispatch, grad_returned, preferred_element_type=jnp.float32).astype(
        jnp.bfloat16
    )
    grad_arrived = to_owners(grad_sent.reshape(owners, expert_local, capacity, width))
    grad_rows = spread_rows(grad_arrived)
    grad_active = jnp.einsum(
        "sjcd,jfd->sjcf", grad_rows, weight_out, preferred_element_type=jnp.float32
    )
    grad_weight_out = jnp.einsum(
        "sjcf,sjcd->jfd", active, grad_rows, preferred_element_type=jnp.float32
    )
    grad_inner = active_back(grad_active)[0].astype(jnp.bfloat16)
    grad_weight_in = jnp.einsum(
        "sjcd,sjcf->jdf", rows_all, grad_inner, preferred_element_type=jnp.float32
    )
    grad_rows_in = jnp.einsum(
        "sjcf,jdf->sjcd", grad_inner, weight_in, preferred_element_type=jnp.float32
    )
    grad_input_rows = collect_rows(grad_rows_in)
    expert_in_grad, expert_out_grad = (grad_weight_in, grad_weight_out)
    grad_back_rows = to_sources(grad_input_rows.astype(jnp.bfloat16)).reshape(
        experts_all * capacity, width
    )
    grad_normed_two = grad_normed_two + jnp.einsum(
        "st,sd->td", dispatch, grad_back_rows, preferred_element_type=jnp.float32
    )
    grad_middle, grad_gain_two = norm_two_back(grad_normed_two)
    grad_middle = grad_middle + upstream
    grad_attn = grad_middle.astype(jnp.bfloat16)
    grad_mix = transposed_times(mixed, grad_attn)
    grad_mixed = times_transposed(grad_attn, weight_mix).astype(jnp.bfloat16)
    grad_heads = to_heads(grad_mixed.reshape(tokens, 1, width)).reshape(
        full_len, heads_local, HEAD_DIM
    )
    grad_query = []
    grad_keys = jnp.zeros((full_len, heads_local, HEAD_DIM), jnp.float32)
    grad_values = jnp.zeros((full_len, heads_local, HEAD_DIM), jnp.float32)
    for number, start in enumerate(starts):
        reach = full_len
        block_query = query[start : start + QBLOCK]
        scores = masked_scores(block_query, keys, start, length, scale)
        probs = jnp.exp(scores - totals[number])
        probs_low = probs.astype(jnp.bfloat16)
        grad_out = grad_heads[start : start + QBLOCK]
        grad_values = grad_values.at[:reach].add(
            jnp.einsum("hqk,qhd->khd", probs_low, grad_out, preferred_element_type=jnp.float32)
        )
        grad_probs = jnp.einsum(
            "qhd,khd->hqk", grad_out, values, preferred_element_type=jnp.float32
        )
        grad_scores = (
            probs * (grad_probs - jnp.sum(grad_probs * probs, axis=-1, keepdims=True))
        ).astype(jnp.bfloat16)
        grad_query.append(
            jnp.einsum("hqk,khd->qhd", grad_scores, keys, preferred_element_type=jnp.float32)
            * scale
        )
        grad_keys = grad_keys.at[:reach].add(
            jnp.einsum("hqk,qhd->khd", grad_scores, block_query, preferred_element_type=jnp.float32)
            * scale
        )
    grad_grouped = jnp.stack([jnp.concatenate(grad_query, axis=0), grad_keys, grad_values], axis=1)
    grad_grouped = grad_grouped.astype(jnp.bfloat16).reshape(full_len, 3, group_width)
    grad_projected = to_tokens(grad_grouped).reshape(tokens, 3 * width)
    grad_qkv_weight = transposed_times(normed, grad_projected)
    grad_normed = times_transposed(grad_projected, weight_qkv)
    grad_inputs, grad_gain_one = norm_back(grad_normed)
    grad_inputs = grad_inputs + grad_middle
    gain_one_grad, qkv_weight_grad, mix_grad, gain_two_grad, route_grad = (
        lax.psum_scatter(grad_gain_one, ("seq", "fsdp"), scatter_dimension=0, tiled=True),
        lax.psum_scatter(grad_qkv_weight, ("seq", "fsdp"), scatter_dimension=0, tiled=True),
        lax.psum_scatter(grad_mix, ("seq", "fsdp"), scatter_dimension=0, tiled=True),
        lax.psum_scatter(grad_gain_two, ("seq", "fsdp"), scatter_dimension=0, tiled=True),
        lax.psum_scatter(grad_route, ("seq", "fsdp"), scatter_dimension=0, tiled=True),
    )
    return (
        output.astype(jnp.bfloat16)[None],
        grad_inputs[None],
        gain_one_grad,
        qkv_weight_grad,
        mix_grad,
        gain_two_grad,
        route_grad,
        expert_in_grad,
        expert_out_grad,
    )


def solution(mesh):
    placed = (
        P("fsdp", "seq", None),
        P("fsdp"),
        P("fsdp", "seq", None),
        P(("seq", "fsdp")),
        P(("seq", "fsdp"), None),
        P(("seq", "fsdp"), None),
        P(("seq", "fsdp")),
        P(("seq", "fsdp"), None),
        P("fsdp", None, "seq"),
        P("fsdp", "seq", None),
        P("fsdp", "seq", None),
    )
    return jax.shard_map(
        shards,
        mesh=mesh,
        in_specs=placed,
        out_specs=(
            P("fsdp", "seq", None),
            P("fsdp", "seq", None),
            P(("seq", "fsdp")),
            P(("seq", "fsdp"), None),
            P(("seq", "fsdp"), None),
            P(("seq", "fsdp")),
            P(("seq", "fsdp"), None),
            P("fsdp", None, "seq"),
            P("fsdp", "seq", None),
        ),
        check_vma=False,
    )
```

profile of v0, /device:TPU:0, one launch (start us, length us, event | category | flops | bytes accessed | tf_op | source)
XLA Modules:
  0.0 1116.4 jit_solution(15297391344962001983)
XLA Ops:
  9.6 43.1 %all-reduce.5 = (bf16[1024]{0:T(1024)(128)(2,1)S(1)}, bf16[1024]{0:T(1024)(128)(2,1)S(1)}) all-reduce(bf16[1024]{0:T(1024)(128)(2,1)S(1)} %dynamic-update-slice.8, bf16[1024]{0:T(1024)(128)(2,1)S(1)} %dynamic-update-slice.9), channel_id=1, replica_groups=mesh['seq'=4,'fsdp'=8] {'seq','fsdp'}, use_global_device_ids=true, to_apply=%add | all-reduce | flops 2048 | bytes 8192
  53.9 29.5 %all-gather.6.cloned.1.call-done = bf16[1024,3072]{1,0:T(8,128)(2,1)} async-done(((bf16[32,3072]{1,0:T(8,128)(2,1)}), bf16[1024,3072]{1,0:T(8,128)(2,1)}) %all-gather.6.cloned.1.call-update) | async-done | bytes 6291472 | tf_op jit(solution)/shard_map/all_gather | solution.py:86
  97.9 23.4 %all-to-all-done = bf16[256,3,1024]{0,1,2:T(4,128)(2,1)S(1)} async-done(((bf16[256,3,1024]{0,1,2:T(4,128)(2,1)}), bf16[256,3,1024]{0,1,2:T(4,128)(2,1)S(1)}, u32[]{:S(2)}, u32[]{:S(2)}) %all-to-all-start) | async-done | bytes 1572896 | tf_op jit(solution)/shard_map/all_to_all | solution.py:33
  150.0 10.3 all-to-all-done.1
  171.3 29.9 %all_to_all.83 = bf16[8,2,32,1024]{3,2,1,0:T(8,128)(2,1)S(1)} all-to-all(bf16[8,2,32,1024]{3,2,1,0:T(8,128)(2,1)S(1)} %bitcast.238), channel_id=1, replica_groups=mesh['seq'=4,'fsdp'=8] {'fsdp'}, dimensions={0} | all-to-all | bytes 2097152 | tf_op jit(solution)/shard_map/all_to_all | solution.py:41
  202.4 49.8 %all-gather.10.cloned.1.call-done = bf16[8,2,128,1024]{3,2,0,1:T(8,128)(2,1)} async-done(((bf16[8,2,32,1024]{3,2,0,1:T(8,128)(2,1)}), bf16[8,2,128,1024]{3,2,0,1:T(8,128)(2,1)}) %all-gather.10.cloned.1.call-update) | async-done | bytes 4194320 | tf_op jit(solution)/shard_map/all_gather | solution.py:49
  270.5 86.6 %reduce-scatter.8.cloned.1.call-done = f32[8,2,32,1024]{3,2,0,1:T(8,128)} async-done(((f32[8,2,128,1024]{3,2,0,1:T(8,128)}), f32[8,2,32,1024]{3,2,0,1:T(8,128)}) %reduce-scatter.8.cloned.1.call-update) | async-done | bytes 2097168 | tf_op jit(solution)/shard_map/reduce_scatter | solution.py:53
  364.5 56.3 %all-gather = bf16[32,32,16]{1,2,0:T(8,128)(2,1)S(1)} all-gather(bf16[1,32,16]{1,2,0:T(8,128)(2,1)S(1)} %bitcast.256), channel_id=1, replica_groups=mesh['seq'=4,'fsdp'=8] {'seq','fsdp'}, dimensions={0}, use_global_device_ids=true | all-gather | bytes 33792 | tf_op jit(solution)/shard_map/all_gather | solution.py:89
  427.4 29.0 %all_to_all.84 = bf16[8,2,32,1024]{3,2,1,0:T(8,128)(2,1)S(1)} all-to-all(bf16[8,2,32,1024]{3,2,1,0:T(8,128)(2,1)S(1)} %bitcast.248), channel_id=1, replica_groups=mesh['seq'=4,'fsdp'=8] {'fsdp'}, dimensions={0} | all-to-all | bytes 2097152 | tf_op jit(solution)/shard_map/all_to_all | solution.py:41
  458.1 50.1 %all-gather.12.cloned.1.call-done = bf16[8,2,128,1024]{3,2,0,1:T(8,128)(2,1)} async-done(((bf16[8,2,32,1024]{3,2,0,1:T(8,128)(2,1)}), bf16[8,2,128,1024]{3,2,0,1:T(8,128)(2,1)}) %all-gather.12.cloned.1.call-update) | async-done | bytes 4194320 | tf_op jit(solution)/shard_map/all_gather | solution.py:49
  508.2 13.4 %fusion.6 = bf16[8,2,128,1024]{3,2,0,1:T(8,128)(2,1)S(1)} fusion(f32[2,8,128,1024]{3,2,1,0:T(8,128)} %copy-done.38, bf16[8,2,128,1024]{3,2,0,1:T(8,128)(2,1)} %all-gather.12.cloned.1.call-done, bf16[2,1024,1024]{2,1,0:T(8,128)(2,1)} %param.36), kind=kOutput, calls=%fused_computation.8 | convolution fusion | flops 4336910336 | bytes 20971520 | tf_op jit(solution)/shard_map/sjcd,jfd->sjcf/dot_general | solution.py:166
  530.5 86.5 %reduce-scatter.10.cloned.1.call-done = f32[8,2,32,1024]{3,2,0,1:T(8,128)} async-done(((f32[8,2,128,1024]{3,2,0,1:T(8,128)}), f32[8,2,32,1024]{3,2,0,1:T(8,128)}) %reduce-scatter.10.cloned.1.call-update) | async-done | bytes 2097168 | tf_op jit(solution)/shard_map/reduce_scatter | solution.py:53
  625.1 26.3 %all-to-all-done.5 = bf16[8,2,32,1024]{3,2,1,0:T(8,128)(2,1)} async-done(((bf16[8,2,32,1024]{3,2,1,0:T(8,128)(2,1)}), bf16[8,2,32,1024]{3,2,1,0:T(8,128)(2,1)}, u32[]{:S(2)}, u32[]{:S(2)}) %all-to-all-start.5) | async-done | bytes 1048608 | tf_op jit(solution)/shard_map/all_to_all | solution.py:45
  696.4 7.8 multiply_reduce_fusion
  704.2 7.7 multiply_reduce_fusion.1
  712.4 8.4 multiply_convert_fusion
  738.9 27.6 %all_to_all.85 = bf16[1024,3,256]{2,1,0:T(4,128)(2,1)S(1)} all-to-all(bf16[1024,3,256]{2,1,0:T(4,128)(2,1)S(1)} %pad_maximum_fusion), channel_id=1, replica_groups=mesh['seq'=4,'fsdp'=8] {'seq'}, dimensions={0} | all-to-all | bytes 3145728 | tf_op jit(solution)/shard_map/all_to_all | solution.py:37
  770.7 7.9 fusion.62
  778.7 29.1 %reduce-scatter.16.cloned.1.call-done = f32[32,16]{1,0:T(8,128)} async-done(((f32[1024,16]{1,0:T(8,128)}), f32[32,16]{1,0:T(8,128)}) %reduce-scatter.16.cloned.1.call-update) | async-done | bytes 2064
  809.2 11.6 %convolution_bitcast_fusion.1 = f32[2,1024,1024]{2,1,0:T(8,128)} fusion(bf16[8,2,128,1024]{3,2,0,1:T(8,128)(2,1)} %all-gather.10.cloned.1.call-done, bf16[8,2,128,1024]{3,2,0,1:T(8,128)(2,1)} %copy-done.39), kind=kOutput, calls=%fused_computation.41 | convolution fusion | flops 4294967296 | bytes 16777216 | tf_op jit(solution)/shard_map/sjcd,sjcf->jdf/dot_general | solution.py:173
  820.7 12.4 %convolution_bitcast_fusion = f32[2,1024,1024]{2,1,0:T(8,128)} fusion(bf16[8,2,128,1024]{3,2,0,1:T(8,128)(2,1)S(1)} %copy-done.37, f32[2,8,128,1024]{3,2,1,0:T(8,128)} %copy-done.38), kind=kOutput, calls=%fused_computation.40 | convolution fusion | flops 4313841664 | bytes 20971520 | tf_op jit(solution)/shard_map/sjcf,sjcd->jfd/dot_general | solution.py:169
  835.7 37.6 %all-reduce.4 = (f32[1024]{0:T(1024)S(1)}, f32[1024]{0:T(1024)S(1)}) all-reduce(f32[1024]{0:T(1024)S(1)} %get-tuple-element.91, f32[1024]{0:T(1024)S(1)} %get-tuple-element.89), channel_id=4, replica_groups=mesh['seq'=4,'fsdp'=8] {'seq','fsdp'}, use_global_device_ids=true, to_apply=%region_21.22.clone | all-reduce | flops 2048 | bytes 16384
  875.7 74.1 %reduce-scatter.14.cloned.1.call-done = f32[32,1024]{1,0:T(8,128)} async-done(((f32[1024,1024]{1,0:T(8,128)}), f32[32,1024]{1,0:T(8,128)}) %reduce-scatter.14.cloned.1.call-update) | async-done | bytes 131088 | tf_op jit(solution)/shard_map/reduce_scatter | solution.py:232
  949.8 159.9 %reduce-scatter.12.cloned.1.call-done = f32[32,3072]{1,0:T(8,128)} async-done(((f32[1024,3072]{1,0:T(8,128)}), f32[32,3072]{1,0:T(8,128)}) %reduce-scatter.12.cloned.1.call-update) | async-done | bytes 393232 | tf_op jit(solution)/shard_map/reduce_scatter | solution.py:231
  (225 shorter events, 182.6 us)
Async XLA Ops:
  7.2 76.3 %all-gather.6.cloned.1.call-start = ((), (), s32[]{:S(2)}) async-start(), calls=%async_computation.13 | async-start | bytes 6488064 | tf_op jit(solution)/shard_map/all_gather | solution.py:86
  91.7 29.6 %all-to-all-start = ((bf16[256,3,1024]{0,1,2:T(4,128)(2,1)}), bf16[256,3,1024]{0,1,2:T(4,128)(2,1)S(1)}, u32[]{:S(2)}, u32[]{:S(2)}) async-start(bf16[256,3,1024]{0,1,2:T(4,128)(2,1)} %copy.83), calls=%async_computation | async-start | bytes 4194304 | tf_op jit(solution)/shard_map/all_to_all | solution.py:33
  95.3 72.9 %all-gather.8.cloned.1.call-start = ((), (), s32[]{:S(2)}) async-start(), calls=%async_computation.14 | async-start | bytes 2162688 | tf_op jit(solution)/shard_map/all_gather | solution.py:87
  145.8 14.4 %all-to-all-start.1 = ((bf16[4,2,32768]{2,1,0:T(2,128)(2,1)}), bf16[4,2,32768]{2,1,0:T(2,128)(2,1)S(1)}, u32[]{:S(2)}, u32[]{:S(2)}) async-start(bf16[4,2,32768]{2,1,0:T(2,128)(2,1)} %reshape.434), calls=%async_computation.1 | async-start | bytes 1048576 | tf_op jit(solution)/shard_map/all_to_all | solution.py:37
  149.3 102.9 %all-gather.10.cloned.1.call-start = ((), (), s32[]{:S(2)}) async-start(), calls=%async_computation.15 | async-start | bytes 5242880 | tf_op jit(solution)/shard_map/all_gather | solution.py:49
  162.9 97.0 %copy-start.14 = (bf16[256,1,4,256]{0,3,2,1:T(8,128)(2,1)}, bf16[256,1,4,256]{0,3,2,1:T(8,128)(2,1)S(1)}, u32[]{:S(2)}) copy-start(bf16[256,1,4,256]{0,3,2,1:T(8,128)(2,1)S(1)} %copy.91) | copy-start | bytes 1572868
  170.6 89.3 %copy-start.32 = (f32[256]{0:T(256)}, f32[256]{0:T(256)S(1)}, u32[]{:S(2)}) copy-start(f32[256]{0:T(256)S(1)} %get-tuple-element.113) | copy-start | bytes 3076
  170.8 250.8 %copy-start.10 = (bf16[256,1024]{1,0:T(8,128)(2,1)}, bf16[256,1024]{1,0:T(8,128)(2,1)S(1)}, u32[]{:S(2)}) copy-start(bf16[256,1024]{1,0:T(8,128)(2,1)S(1)} %multiply_convert_fusion.3) | copy-start | bytes 1572868
  202.3 154.7 %reduce-scatter.8.cloned.1.call-start = ((), (), s32[]{:S(2)}) async-start(), calls=%async_computation.16 | async-start | bytes 10485760 | tf_op jit(solution)/shard_map/reduce_scatter | solution.py:53
  270.4 94.1 %copy-start.34 = (bf16[32,16]{0,1:T(8,128)(2,1)S(1)}, bf16[32,16]{0,1:T(8,128)(2,1)}, u32[]{:S(2)}) copy-start(bf16[32,16]{0,1:T(8,128)(2,1)} %param.34) | copy-start | bytes 3076
  270.4 152.3 %copy-start.18 = (bf16[1,256,1024]{2,1,0:T(8,128)(2,1)S(1)}, bf16[1,256,1024]{2,1,0:T(8,128)(2,1)}, u32[]{:S(2)}) copy-start(bf16[1,256,1024]{2,1,0:T(8,128)(2,1)} %param.37) | copy-start | bytes 1572868
  359.9 62.9 %all-to-all-start.3 = ((bf16[8,2,32,1024]{3,2,1,0:T(8,128)(2,1)}), bf16[8,2,32,1024]{3,2,1,0:T(8,128)(2,1)}, u32[]{:S(2)}, u32[]{:S(2)}) async-start(bf16[8,2,32,1024]{3,2,1,0:T(8,128)(2,1)} %copy.95), calls=%async_computation.4 | async-start | bytes 2097152 | tf_op jit(solution)/shard_map/all_to_all | solution.py:45
  364.5 143.7 %all-gather.12.cloned.1.call-start = ((), (), s32[]{:S(2)}) async-start(), calls=%async_computation.17 | async-start | bytes 5242880 | tf_op jit(solution)/shard_map/all_gather | solution.py:49
  457.5 159.6 %reduce-scatter.10.cloned.1.call-start = ((), (), s32[]{:S(2)}) async-start(), calls=%async_computation.18 | async-start | bytes 10485760 | tf_op jit(solution)/shard_map/reduce_scatter | solution.py:53
  530.5 94.3 %copy-start.19 = (bf16[1024,16]{0,1:T(8,128)(2,1)S(1)}, bf16[1024,16]{0,1:T(8,128)(2,1)}, u32[]{:S(2)}) copy-start(bf16[1024,16]{0,1:T(8,128)(2,1)} %reshape.426) | copy-start | bytes 98308
  530.5 94.3 %copy-start.23 = (s32[1,256,1]{1,2,0:T(1,128)S(1)}, s32[1,256,1]{1,2,0:T(1,128)}, u32[]{:S(2)}) copy-start(s32[1,256,1]{1,2,0:T(1,128)} %param.29) | copy-start | bytes 3076
  530.5 120.9 %copy-start.25 = (s32[256]{0:T(256)S(1)}, s32[256]{0:T(256)}, u32[]{:S(2)}) copy-start(s32[256]{0:T(256)} %copy-done.24) | copy-start | bytes 3076
  530.5 120.9 %copy-start.27 = (f32[256]{0:T(256)S(1)}, f32[256]{0:T(256)}, u32[]{:S(2)}) copy-start(f32[256]{0:T(256)} %copy-done.26) | copy-start | bytes 3076
  530.5 122.9 %copy-start.33 = (f32[256]{0:T(256)S(1)}, f32[256]{0:T(256)}, u32[]{:S(2)}) copy-start(f32[256]{0:T(256)} %copy-done.32) | copy-start | bytes 3076
  619.9 31.5 %all-to-all-start.5 = ((bf16[8,2,32,1024]{3,2,1,0:T(8,128)(2,1)}), bf16[8,2,32,1024]{3,2,1,0:T(8,128)(2,1)}, u32[]{:S(2)}, u32[]{:S(2)}) async-start(bf16[8,2,32,1024]{3,2,1,0:T(8,128)(2,1)} %copy.97), calls=%async_computation.7 | async-start | bytes 2097152 | tf_op jit(solution)/shard_map/all_to_all | solution.py:45
  666.7 12.3 %all-to-all-start.6 = ((bf16[4,2,32768]{2,1,0:T(2,128)(2,1)}), bf16[4,2,32768]{2,1,0:T(2,128)(2,1)}, u32[]{:S(2)}, u32[]{:S(2)}) async-start(bf16[4,2,32768]{2,1,0:T(2,128)(2,1)} %reshape.436), calls=%async_computation.8 | async-start | bytes 1048576 | tf_op jit(solution)/shard_map/all_to_all | solution.py:33
  670.8 136.9 %reduce-scatter.16.cloned.1.call-start = ((), (), s32[]{:S(2)}) async-start(), calls=%async_computation.21 | async-start | bytes 540672
  673.1 276.7 %reduce-scatter.14.cloned.1.call-start = ((), (), s32[]{:S(2)}) async-start(), calls=%async_computation.20 | async-start | bytes 4325376 | tf_op jit(solution)/shard_map/reduce_scatter | solution.py:232
  676.9 432.9 %reduce-scatter.12.cloned.1.call-start = ((), (), s32[]{:S(2)}) async-start(), calls=%async_computation.19 | async-start | bytes 12976128 | tf_op jit(solution)/shard_map/reduce_scatter | solution.py:231
  (36 other events, 593.7 us)
Sparse Core Ops, SparseCore 0:
  11.0 72.3 all-gather.5
  99.1 69.0 all-gather.7
  202.4 49.7 all-gather.9
  270.6 86.4 reduce-scatter.7
  457.6 50.5 all-gather.11
  530.6 86.3 reduce-scatter.9
  673.9 133.8 reduce-scatter.15
  810.7 139.0 reduce-scatter.13
  957.5 152.2 reduce-scatter.11
where the time goes:
time: 1120 us
  waiting for transfers between devices  634 us (57%)
  blocking collectives  224 us (20%)
  matrix products  133 us (12%)
  local copies, waits for them, and re-layouts  53.2 us (5%)
  other arithmetic  34.8 us (3%)
  starting transfers between devices  22.3 us (2%)
  between operations  15.5 us (1%)
    reduce_scatter x2, waiting for transfers between devices, collect_rows(): return lax.psum_scatter(value, 'seq', scatter_dimension=2, tiled=True)  173 us
    reduce_scatter x1, waiting for transfers between devices, shards(): lax.psum_scatter(grad_qkv_weight, ('seq', 'fsdp'), scatter_dimension=0, t...  160 us
    all_gather x2, waiting for transfers between devices, spread_rows(): return lax.all_gather(value, 'seq', axis=2, tiled=True)  99.9 us
    unnamed x2, blocking collectives  80.7 us
    reduce_scatter x1, waiting for transfers between devices, shards(): lax.psum_scatter(grad_mix, ('seq', 'fsdp'), scatter_dimension=0, tiled=True)  74.1 us
    all_to_all x2, blocking collectives, to_owners(): lax.all_to_all(value, 'fsdp', split_axis=0, concat_axis=0, tiled=True)  59 us
    all_gather x1, blocking collectives, shards(): lax.all_gather(router_weight, ('seq', 'fsdp'), axis=0, tiled=True)  56.3 us
    unnamed x10, waiting for transfers between devices  30.3 us
  transfers between devices with their start and end apart: 14, of which 13 were waited for; matrix products, arithmetic and copies ran while one was open for 12% of the time, Pallas kernels for 0%

commit v1 on v0

--- a/solution.py
+++ b/solution.py
@@ -9,6 +9,28 @@
 MASKED = -1e30
 
 
+def laid_out(pieces, dim):
+    pieces = jnp.moveaxis(pieces, 0, dim)
+    shape = pieces.shape
+    return pieces.reshape(*shape[:dim], shape[dim] * shape[dim + 1], *shape[dim + 2 :])
+
+
+def collect(array, axis, dim):
+    count = lax.axis_size(axis)
+    pairs = [(i, (i + 1) % count) for i in range(count)]
+    back = [(b, a) for a, b in pairs]
+    lower, upper = ([], [])
+    for hop in range(count - 1):
+        if hop % 2 == 0:
+            lower.append(lax.ppermute(lower[-1] if lower else array, axis, pairs))
+        else:
+            upper.append(lax.ppermute(upper[-1] if upper else array, axis, back))
+    blocks = jnp.stack([*lower[::-1], array, *upper])
+    shift = lax.axis_index(axis) - len(lower)
+    blocks = blocks[(jnp.arange(count) - shift) % count]
+    return laid_out(blocks, dim)
+
+
 def scaled_norm(value, gain):
     return value * lax.rsqrt(jnp.mean(value * value, axis=-1, keepdims=True) + EPS) * gain
 
@@ -46,7 +68,7 @@
 
 
 def spread_rows(value):
-    return lax.all_gather(value, "seq", axis=2, tiled=True)
+    return collect(value, "seq", 2)
 
 
 def collect_rows(value):

time: 1120 us -> 1180 us (1.054)
  waiting for transfers between devices: 634 us -> 664 us
  local copies, waits for them, and re-layouts: 53.2 us -> 70 us
    ppermute x0 -> x6, waiting for transfers between devices: none -> 135 us  [the longest x4 91.5 us: collect(): lower.append(lax.ppermute(lower[-1] if lower else array, axis, pairs))]
    all_gather x2 -> x0, waiting for transfers between devices: 99.9 us -> none  [spread_rows(): return lax.all_gather(value, 'seq', axis=2, tiled=True)]
    unnamed x10 -> x8, waiting for transfers between devices: 30.3 us -> 29.7 us
  transfers between devices with their start and end apart: 14 -> 18, of which waited for: 13 -> 17; matrix products, arithmetic and copies ran while one was open for 12% -> 12% of each run, Pallas kernels for 0% -> 0%
where the time goes in v1:
time: 1180 us; the launch traced here: 1170 us
  waiting for transfers between devices  664 us (56%)
  blocking collectives  224 us (19%)
  matrix products  128 us (11%)
  local copies, waits for them, and re-layouts  70 us (6%)
  other arithmetic  40.9 us (3%)
  starting transfers between devices  27.9 us (2%)
  between operations  15.9 us (1%)
    reduce_scatter x2, waiting for transfers between devices, collect_rows(): return lax.psum_scatter(value, 'seq', scatter_dimension=2, tiled=True)  169 us
    reduce_scatter x1, waiting for transfers between devices, shards(): lax.psum_scatter(grad_qkv_weight, ('seq', 'fsdp'), scatter_dimension=0, t...  160 us
    ppermute x4, waiting for transfers between devices, collect(): lower.append(lax.ppermute(lower[-1] if lower else array, axis, pairs))  91.5 us
    unnamed x2, blocking collectives  80.5 us
    reduce_scatter x1, waiting for transfers between devices, shards(): lax.psum_scatter(grad_mix, ('seq', 'fsdp'), scatter_dimension=0, tiled=True)  74.4 us
    all_to_all x2, blocking collectives, to_owners(): lax.all_to_all(value, 'fsdp', split_axis=0, concat_axis=0, tiled=True)  59.1 us
    all_gather x1, blocking collectives, shards(): lax.all_gather(router_weight, ('seq', 'fsdp'), axis=0, tiled=True)  56.3 us
    ppermute x2, waiting for transfers between devices, collect(): upper.append(lax.ppermute(upper[-1] if upper else array, axis, back))  43.3 us
  transfers between devices with their start and end apart: 18, of which 17 were waited for; matrix products, arithmetic and copies ran while one was open for 12% of the time, Pallas kernels for 0%

profile of v1, /device:TPU:0, one launch (start us, length us, event | category | flops | bytes accessed | tf_op | source)
XLA Modules:
  0.0 1170.4 jit_solution(7351696413192791402)
XLA Ops:
  9.6 43.1 %all-reduce.5 = (bf16[1024]{0:T(1024)(128)(2,1)S(1)}, bf16[1024]{0:T(1024)(128)(2,1)S(1)}) all-reduce(bf16[1024]{0:T(1024)(128)(2,1)S(1)} %dynamic-update-slice.8, bf16[1024]{0:T(1024)(128)(2,1)S(1)} %dynamic-update-slice.9), channel_id=1, replica_groups=mesh['seq'=4,'fsdp'=8] {'seq','fsdp'}, use_global_device_ids=true, to_apply=%add | all-reduce | flops 2048 | bytes 8192
  54.5 29.0 %all-gather.4.cloned.1.call-done = bf16[1024,3072]{1,0:T(8,128)(2,1)} async-done(((bf16[32,3072]{1,0:T(8,128)(2,1)}), bf16[1024,3072]{1,0:T(8,128)(2,1)}) %all-gather.4.cloned.1.call-update) | async-done | bytes 6291472 | tf_op jit(solution)/shard_map/all_gather | solution.py:108
  97.9 23.5 %all-to-all-done = bf16[256,3,1024]{0,1,2:T(4,128)(2,1)S(1)} async-done(((bf16[256,3,1024]{0,1,2:T(4,128)(2,1)}), bf16[256,3,1024]{0,1,2:T(4,128)(2,1)S(1)}, u32[]{:S(2)}, u32[]{:S(2)}) %all-to-all-start) | async-done | bytes 1572896 | tf_op jit(solution)/shard_map/all_to_all | solution.py:55
  149.9 10.4 all-to-all-done.1
  171.2 30.1 %all_to_all.83 = bf16[8,2,32,1024]{3,2,1,0:T(8,128)(2,1)} all-to-all(bf16[8,2,32,1024]{3,2,1,0:T(8,128)(2,1)S(1)} %bitcast.255), channel_id=1, replica_groups=mesh['seq'=4,'fsdp'=8] {'fsdp'}, dimensions={0} | all-to-all | bytes 2097152 | tf_op jit(solution)/shard_map/all_to_all | solution.py:63
  204.2 24.4 %collective-permute-done = bf16[8,2,32,1024]{3,2,1,0:T(8,128)(2,1)} collective-permute-done((bf16[8,2,32,1024]{3,2,1,0:T(8,128)(2,1)}, bf16[8,2,32,1024]{3,2,1,0:T(8,128)(2,1)}, u32[]{:S(2)}, u32[]{:S(2)}) %collective-permute-start) | collective-permute-done | bytes 1048608 | tf_op jit(solution)/shard_map/ppermute | solution.py:25
  228.6 21.4 %collective-permute-done.2 = bf16[8,2,32,1024]{3,2,1,0:T(8,128)(2,1)} collective-permute-done((bf16[8,2,32,1024]{3,2,1,0:T(8,128)(2,1)}, bf16[8,2,32,1024]{3,2,1,0:T(8,128)(2,1)}, u32[]{:S(2)}, u32[]{:S(2)}) %collective-permute-start.2) | collective-permute-done | bytes 1048608 | tf_op jit(solution)/shard_map/ppermute | solution.py:27
  250.0 22.0 %collective-permute-done.1 = bf16[8,2,32,1024]{3,2,1,0:T(8,128)(2,1)} collective-permute-done((bf16[8,2,32,1024]{3,2,1,0:T(8,128)(2,1)}, bf16[8,2,32,1024]{3,2,1,0:T(8,128)(2,1)}, u32[]{:S(2)}, u32[]{:S(2)}) %collective-permute-start.1) | collective-permute-done | bytes 1048608 | tf_op jit(solution)/shard_map/ppermute | solution.py:25
  300.7 84.2 %reduce-scatter.8.cloned.1.call-done = f32[8,2,32,1024]{3,2,0,1:T(8,128)} async-done(((f32[8,2,128,1024]{3,2,0,1:T(8,128)}), f32[8,2,32,1024]{3,2,0,1:T(8,128)}) %reduce-scatter.8.cloned.1.call-update) | async-done | bytes 2097168 | tf_op jit(solution)/shard_map/reduce_scatter | solution.py:75
  392.4 56.3 %all-gather = bf16[32,32,16]{1,2,0:T(8,128)(2,1)S(1)} all-gather(bf16[1,32,16]{1,2,0:T(8,128)(2,1)S(1)} %bitcast.277), channel_id=1, replica_groups=mesh['seq'=4,'fsdp'=8] {'seq','fsdp'}, dimensions={0}, use_global_device_ids=true | all-gather | bytes 33792 | tf_op jit(solution)/shard_map/all_gather | solution.py:111
  455.2 29.0 %all_to_all.84 = bf16[8,2,32,1024]{3,2,1,0:T(8,128)(2,1)S(1)} all-to-all(bf16[8,2,32,1024]{3,2,1,0:T(8,128)(2,1)S(1)} %bitcast.266), channel_id=1, replica_groups=mesh['seq'=4,'fsdp'=8] {'fsdp'}, dimensions={0} | all-to-all | bytes 2097152 | tf_op jit(solution)/shard_map/all_to_all | solution.py:63
  487.1 24.1 %collective-permute-done.3 = bf16[8,2,32,1024]{3,2,1,0:T(8,128)(2,1)S(1)} collective-permute-done((bf16[8,2,32,1024]{3,2,1,0:T(8,128)(2,1)S(1)}, bf16[8,2,32,1024]{3,2,1,0:T(8,128)(2,1)S(1)}, u32[]{:S(2)}, u32[]{:S(2)}) %collective-permute-start.3) | collective-permute-done | bytes 1048608 | tf_op jit(solution)/shard_map/ppermute | solution.py:25
  511.6 22.0 %collective-permute-done.5 = bf16[8,2,32,1024]{3,2,1,0:T(8,128)(2,1)S(1)} collective-permute-done((bf16[8,2,32,1024]{3,2,1,0:T(8,128)(2,1)S(1)}, bf16[8,2,32,1024]{3,2,1,0:T(8,128)(2,1)S(1)}, u32[]{:S(2)}, u32[]{:S(2)}) %collective-permute-start.5) | collective-permute-done | bytes 1048608 | tf_op jit(solution)/shard_map/ppermute | solution.py:27
  533.5 21.0 %collective-permute-done.4 = bf16[8,2,32,1024]{3,2,1,0:T(8,128)(2,1)S(1)} collective-permute-done((bf16[8,2,32,1024]{3,2,1,0:T(8,128)(2,1)S(1)}, bf16[8,2,32,1024]{3,2,1,0:T(8,128)(2,1)S(1)}, u32[]{:S(2)}, u32[]{:S(2)}) %collective-permute-start.4) | collective-permute-done | bytes 1048608 | tf_op jit(solution)/shard_map/ppermute | solution.py:25
  565.4 12.2 %fusion.6 = bf16[8,2,128,1024]{3,2,0,1:T(8,128)(2,1)S(1)} fusion(f32[2,8,128,1024]{3,2,1,0:T(8,128)} %copy-done.45, bf16[8,2,128,1024]{3,2,0,1:T(8,128)(2,1)S(1)} %bitcast.252, bf16[2,1024,1024]{2,1,0:T(8,128)(2,1)S(1)} %copy-done.42), kind=kOutput, calls=%fused_computation.10 | convolution fusion | flops 4336910336 | bytes 20971520 | tf_op jit(solution)/shard_map/sjcd,jfd->sjcf/dot_general | solution.py:188
  586.5 84.9 %reduce-scatter.10.cloned.1.call-done = f32[8,2,32,1024]{3,2,0,1:T(8,128)} async-done(((f32[8,2,128,1024]{3,2,0,1:T(8,128)}), f32[8,2,32,1024]{3,2,0,1:T(8,128)}) %reduce-scatter.10.cloned.1.call-update) | async-done | bytes 2097168 | tf_op jit(solution)/shard_map/reduce_scatter | solution.py:75
  679.3 26.3 %all-to-all-done.5 = bf16[8,2,32,1024]{3,2,1,0:T(8,128)(2,1)} async-done(((bf16[8,2,32,1024]{3,2,1,0:T(8,128)(2,1)}), bf16[8,2,32,1024]{3,2,1,0:T(8,128)(2,1)}, u32[]{:S(2)}, u32[]{:S(2)}) %all-to-all-start.5) | async-done | bytes 1048608 | tf_op jit(solution)/shard_map/all_to_all | solution.py:67
  793.2 27.7 %all_to_all.85 = bf16[1024,3,256]{2,1,0:T(4,128)(2,1)S(1)} all-to-all(bf16[1024,3,256]{2,1,0:T(4,128)(2,1)S(1)} %pad_maximum_fusion.2), channel_id=1, replica_groups=mesh['seq'=4,'fsdp'=8] {'seq'}, dimensions={0} | all-to-all | bytes 3145728 | tf_op jit(solution)/shard_map/all_to_all | solution.py:59
  833.0 28.8 %reduce-scatter.16.cloned.1.call-done = f32[32,16]{1,0:T(8,128)} async-done(((f32[1024,16]{1,0:T(8,128)}), f32[32,16]{1,0:T(8,128)}) %reduce-scatter.16.cloned.1.call-update) | async-done | bytes 2064
  863.2 11.6 fusion.25
  874.8 12.4 %convolution_bitcast_fusion = f32[2,1024,1024]{2,1,0:T(8,128)} fusion(bf16[8,2,128,1024]{3,2,0,1:T(8,128)(2,1)S(1)} %bitcast.253, f32[2,8,128,1024]{3,2,1,0:T(8,128)} %copy-done.45), kind=kOutput, calls=%fused_computation.48 | convolution fusion | flops 4313841664 | bytes 20971520 | tf_op jit(solution)/shard_map/sjcf,sjcd->jfd/dot_general | solution.py:191
  889.5 37.4 %all-reduce.4 = (f32[1024]{0:T(1024)S(1)}, f32[1024]{0:T(1024)S(1)}) all-reduce(f32[1024]{0:T(1024)S(1)} %get-tuple-element.91, f32[1024]{0:T(1024)S(1)} %get-tuple-element.89), channel_id=4, replica_groups=mesh['seq'=4,'fsdp'=8] {'seq','fsdp'}, use_global_device_ids=true, to_apply=%region_21.22.clone | all-reduce | flops 2048 | bytes 16384
  929.4 74.4 %reduce-scatter.14.cloned.1.call-done = f32[32,1024]{1,0:T(8,128)} async-done(((f32[1024,1024]{1,0:T(8,128)}), f32[32,1024]{1,0:T(8,128)}) %reduce-scatter.14.cloned.1.call-update) | async-done | bytes 131088 | tf_op jit(solution)/shard_map/reduce_scatter | solution.py:254
  1003.7 159.5 %reduce-scatter.12.cloned.1.call-done = f32[32,3072]{1,0:T(8,128)} async-done(((f32[1024,3072]{1,0:T(8,128)}), f32[32,3072]{1,0:T(8,128)}) %reduce-scatter.12.cloned.1.call-update) | async-done | bytes 393232 | tf_op jit(solution)/shard_map/reduce_scatter | solution.py:253
  (251 shorter events, 239.1 us)
Async XLA Ops:
  7.2 76.3 %all-gather.4.cloned.1.call-start = ((), (), s32[]{:S(2)}) async-start(), calls=%async_computation.13 | async-start | bytes 6488064 | tf_op jit(solution)/shard_map/all_gather | solution.py:108
  91.7 29.6 %all-to-all-start = ((bf16[256,3,1024]{0,1,2:T(4,128)(2,1)}), bf16[256,3,1024]{0,1,2:T(4,128)(2,1)S(1)}, u32[]{:S(2)}, u32[]{:S(2)}) async-start(bf16[256,3,1024]{0,1,2:T(4,128)(2,1)} %copy.91), calls=%async_computation | async-start | bytes 4194304 | tf_op jit(solution)/shard_map/all_to_all | solution.py:55
  95.3 72.9 %all-gather.6.cloned.1.call-start = ((), (), s32[]{:S(2)}) async-start(), calls=%async_computation.14 | async-start | bytes 2162688 | tf_op jit(solution)/shard_map/all_gather | solution.py:109
  145.8 14.4 %all-to-all-start.1 = ((bf16[4,2,32768]{2,1,0:T(2,128)(2,1)}), bf16[4,2,32768]{2,1,0:T(2,128)(2,1)S(1)}, u32[]{:S(2)}, u32[]{:S(2)}) async-start(bf16[4,2,32768]{2,1,0:T(2,128)(2,1)} %reshape.507), calls=%async_computation.1 | async-start | bytes 1048576 | tf_op jit(solution)/shard_map/all_to_all | solution.py:59
  149.3 235.6 %reduce-scatter.8.cloned.1.call-start = ((), (), s32[]{:S(2)}) async-start(), calls=%async_computation.15 | async-start | bytes 10485760 | tf_op jit(solution)/shard_map/reduce_scatter | solution.py:75
  149.7 126.1 %copy-start.25 = (f32[1024]{0:T(1024)}, f32[1024]{0:T(1024)S(1)}, u32[]{:S(2)}) copy-start(f32[1024]{0:T(1024)S(1)} %convert_element_type.121) | copy-start | bytes 12292
  149.9 125.9 %copy-start.29 = (s32[256]{0:T(256)}, s32[256]{0:T(256)S(1)}, u32[]{:S(2)}) copy-start(s32[256]{0:T(256)S(1)} %add_add_fusion.2) | copy-start | bytes 3076
  170.8 278.7 %copy-start.10 = (bf16[256,1024]{1,0:T(8,128)(2,1)}, bf16[256,1024]{1,0:T(8,128)(2,1)S(1)}, u32[]{:S(2)}) copy-start(bf16[256,1024]{1,0:T(8,128)(2,1)S(1)} %multiply_convert_fusion.3) | copy-start | bytes 1572868
  201.3 27.3 %collective-permute-start = (bf16[8,2,32,1024]{3,2,1,0:T(8,128)(2,1)}, bf16[8,2,32,1024]{3,2,1,0:T(8,128)(2,1)}, u32[]{:S(2)}, u32[]{:S(2)}) collective-permute-start(bf16[8,2,32,1024]{3,2,1,0:T(8,128)(2,1)} %all_to_all.83), channel_id=1, source_target_pairs={{0,8},{8,16},{16,24},{24,0},{1,9},{9,17},{17,25},{25,1},{2,10},{10... | collective-permute-start | bytes 3145736 | tf_op jit(solution)/shard_map/ppermute | solution.py:25
  201.3 48.7 %collective-permute-start.2 = (bf16[8,2,32,1024]{3,2,1,0:T(8,128)(2,1)}, bf16[8,2,32,1024]{3,2,1,0:T(8,128)(2,1)}, u32[]{:S(2)}, u32[]{:S(2)}) collective-permute-start(bf16[8,2,32,1024]{3,2,1,0:T(8,128)(2,1)} %all_to_all.83), channel_id=1, source_target_pairs={{8,0},{16,8},{24,16},{0,24},{9,1},{17,9},{25,17},{1,25},{10,2},{18... | collective-permute-start | bytes 3145736 | tf_op jit(solution)/shard_map/ppermute | solution.py:27
  228.6 43.4 %collective-permute-start.1 = (bf16[8,2,32,1024]{3,2,1,0:T(8,128)(2,1)}, bf16[8,2,32,1024]{3,2,1,0:T(8,128)(2,1)}, u32[]{:S(2)}, u32[]{:S(2)}) collective-permute-start(bf16[8,2,32,1024]{3,2,1,0:T(8,128)(2,1)} %collective-permute-done), channel_id=1, source_target_pairs={{0,8},{8,16},{16,24},{24,0},{1,9},{9,17},{17,25},{25,1},{2,10},{10... | collective-permute-start | bytes 3145736 | tf_op jit(solution)/shard_map/ppermute | solution.py:25
  300.6 149.9 %copy-start.21 = (bf16[1,256,1024]{2,1,0:T(8,128)(2,1)S(1)}, bf16[1,256,1024]{2,1,0:T(8,128)(2,1)}, u32[]{:S(2)}) copy-start(bf16[1,256,1024]{2,1,0:T(8,128)(2,1)} %param.37) | copy-start | bytes 1572868
  387.7 62.9 %all-to-all-start.3 = ((bf16[8,2,32,1024]{3,2,1,0:T(8,128)(2,1)}), bf16[8,2,32,1024]{3,2,1,0:T(8,128)(2,1)}, u32[]{:S(2)}, u32[]{:S(2)}) async-start(bf16[8,2,32,1024]{3,2,1,0:T(8,128)(2,1)} %copy.104), calls=%async_computation.4 | async-start | bytes 2097152 | tf_op jit(solution)/shard_map/all_to_all | solution.py:67
  392.3 279.2 %reduce-scatter.10.cloned.1.call-start = ((), (), s32[]{:S(2)}) async-start(), calls=%async_computation.16 | async-start | bytes 10485760 | tf_op jit(solution)/shard_map/reduce_scatter | solution.py:75
  484.2 27.0 %collective-permute-start.3 = (bf16[8,2,32,1024]{3,2,1,0:T(8,128)(2,1)S(1)}, bf16[8,2,32,1024]{3,2,1,0:T(8,128)(2,1)S(1)}, u32[]{:S(2)}, u32[]{:S(2)}) collective-permute-start(bf16[8,2,32,1024]{3,2,1,0:T(8,128)(2,1)S(1)} %all_to_all.84), channel_id=1, source_target_pairs={{0,8},{8,16},{16,24},{24,0},{1,9},{9,17},{17,25},{25,1},{2,10},{10... | collective-permute-start | bytes 3145736 | tf_op jit(solution)/shard_map/ppermute | solution.py:25
  484.2 49.4 %collective-permute-start.5 = (bf16[8,2,32,1024]{3,2,1,0:T(8,128)(2,1)S(1)}, bf16[8,2,32,1024]{3,2,1,0:T(8,128)(2,1)S(1)}, u32[]{:S(2)}, u32[]{:S(2)}) collective-permute-start(bf16[8,2,32,1024]{3,2,1,0:T(8,128)(2,1)S(1)} %all_to_all.84), channel_id=1, source_target_pairs={{8,0},{16,8},{24,16},{0,24},{9,1},{17,9},{25,17},{1,25},{10,2},{18... | collective-permute-start | bytes 3145736 | tf_op jit(solution)/shard_map/ppermute | solution.py:27
  511.2 43.4 %collective-permute-start.4 = (bf16[8,2,32,1024]{3,2,1,0:T(8,128)(2,1)S(1)}, bf16[8,2,32,1024]{3,2,1,0:T(8,128)(2,1)S(1)}, u32[]{:S(2)}, u32[]{:S(2)}) collective-permute-start(bf16[8,2,32,1024]{3,2,1,0:T(8,128)(2,1)S(1)} %collective-permute-done.3), channel_id=1, source_target_pairs={{0,8},{8,16},{16,24},{24,0},{1,9},{9,17},{17,25},{25,1},{2,10},{10... | collective-permute-start | bytes 3145736 | tf_op jit(solution)/shard_map/ppermute | solution.py:25
  586.5 119.1 %copy-start.30 = (s32[256]{0:T(256)S(1)}, s32[256]{0:T(256)}, u32[]{:S(2)}) copy-start(s32[256]{0:T(256)} %copy-done.29) | copy-start | bytes 3076
  586.5 121.2 %copy-start.38 = (f32[256]{0:T(256)S(1)}, f32[256]{0:T(256)}, u32[]{:S(2)}) copy-start(f32[256]{0:T(256)} %copy-done.37) | copy-start | bytes 3076
  674.3 31.3 %all-to-all-start.5 = ((bf16[8,2,32,1024]{3,2,1,0:T(8,128)(2,1)}), bf16[8,2,32,1024]{3,2,1,0:T(8,128)(2,1)}, u32[]{:S(2)}, u32[]{:S(2)}) async-start(bf16[8,2,32,1024]{3,2,1,0:T(8,128)(2,1)} %copy.106), calls=%async_computation.7 | async-start | bytes 2097152 | tf_op jit(solution)/shard_map/all_to_all | solution.py:67
  720.9 12.3 %all-to-all-start.6 = ((bf16[4,2,32768]{2,1,0:T(2,128)(2,1)}), bf16[4,2,32768]{2,1,0:T(2,128)(2,1)}, u32[]{:S(2)}, u32[]{:S(2)}) async-start(bf16[4,2,32768]{2,1,0:T(2,128)(2,1)} %reshape.509), calls=%async_computation.8 | async-start | bytes 1048576 | tf_op jit(solution)/shard_map/all_to_all | solution.py:55
  725.1 136.7 %reduce-scatter.16.cloned.1.call-start = ((), (), s32[]{:S(2)}) async-start(), calls=%async_computation.19 | async-start | bytes 540672
  727.4 276.4 %reduce-scatter.14.cloned.1.call-start = ((), (), s32[]{:S(2)}) async-start(), calls=%async_computation.18 | async-start | bytes 4325376 | tf_op jit(solution)/shard_map/reduce_scatter | solution.py:254
  731.1 432.1 %reduce-scatter.12.cloned.1.call-start = ((), (), s32[]{:S(2)}) async-start(), calls=%async_computation.17 | async-start | bytes 12976128 | tf_op jit(solution)/shard_map/reduce_scatter | solution.py:253
  (47 other events, 1385.0 us)
Sparse Core Ops, SparseCore 0:
  11.0 72.3 all-gather.3
  99.1 68.9 all-gather.5
  300.8 84.0 reduce-scatter.7
  586.6 84.7 reduce-scatter.9
  727.9 133.9 reduce-scatter.15
  864.6 139.0 reduce-scatter.13
  1011.4 151.8 reduce-scatter.11
